TPU v7x, 32 devices: a whole 2x2x4 slice. The times are simulated.
32 devices in a mesh: sec: 2 (over core), blk: 16 (over z, y, x).
Axes of the slice: x: 2, y: 2, z: 4, core: 2. Of those that a mesh axis runs over, the one named last changes fastest.
Arguments:
- state: float32 [2, 32, 40, 16384], P('sec', None, None, 'blk'), may hold values from -6 to 6
- diffusion: float32 [2, 40, 16384], P('sec', None, 'blk'), may hold values from 0.05 to 0.25
- transport: float32 [2, 40, 16384], P('sec', None, 'blk'), may hold values from 0.1 to 0.4
- mixing: float32 [2, 40, 40], P('sec'), may hold values from -1 to 1
- src_col: int32 [2, 16, 16, 128], P('sec', 'blk'), may hold values from 0 to 1023
- weights: float32 [2, 16, 16, 128], P('sec', 'blk'), may hold values from 0.05 to 0.25
- counts: int32 [2, 16, 16], P('sec', 'blk'), may hold values from 8 to 128, as said below
- recv_rows: int32 [2, 16, 16, 128], P('sec', 'blk'), may hold values from 0 to 1023
Outputs:
- new_state: float32 [2, 32, 40, 16384], P('sec', None, None, 'blk')
- incoming: float32 [2, 32, 16384], P('sec', None, 'blk')
Inputs may be any that keep to these rules, and one draw needn't show every extreme that they name: `counts`: for each sending component, one destination block drawn from the seed has all 128 slots live from every source block.
All inputs are finite; a program needn't handle non-finite values.
Results may differ from a plain program's by a relative error of at most 0.0003.
Values sent between devices are 32-bit elements; how exact they have to be, the bound alone decides.
A program may use at most 64 MiB of HBM per device.

v0:
```python
import jax
import jax.numpy as jnp
from jax import lax
from jax.sharding import PartitionSpec as P

SUBSTEPS = 2


def padded_2(x, sides, width):
    for axis, dim in sides:
        size, length = (lax.axis_size(axis), x.shape[dim])
        up = [(i, (i + 1) % size) for i in range(size)]
        down = [(j, i) for i, j in up]
        last = lax.slice_in_dim(x, length - width, length, axis=dim)
        leading = lax.slice_in_dim(x, 0, width, axis=dim)
        before = lax.ppermute(last, axis, up)
        after = lax.ppermute(leading, axis, down)
        x = jnp.concatenate([before, x, after], axis=dim)
    return x


def partner(x, axis, apart):
    return lax.ppermute(x, axis, [(i, i ^ 1 << apart) for i in range(lax.axis_size(axis))])


def advance_inner(field, rate_diff, rate_flow):
    left = field[..., :-2]
    middle = field[..., 1:-1]
    right = field[..., 2:]
    return middle + rate_diff * (left - 2.0 * middle + right) + rate_flow * (left - middle)


def split_pieces(values):
    high_part = values.astype(jnp.bfloat16)
    rest = values - lax.optimization_barrier(high_part).astype(jnp.float32)
    middle_part = rest.astype(jnp.bfloat16)
    low_part = (rest - lax.optimization_barrier(middle_part).astype(jnp.float32)).astype(
        jnp.bfloat16
    )
    return (high_part, middle_part, low_part)


def product_sum(values, selector):
    pieces = split_pieces(values)
    total = jnp.dot(pieces[0], selector, preferred_element_type=jnp.float32)
    total = total + jnp.dot(pieces[1], selector, preferred_element_type=jnp.float32)
    return total + jnp.dot(pieces[2], selector, preferred_element_type=jnp.float32)


def body(state, diffusion, transport, mixing, src_col, weights, counts, recv_rows):
    moved = state[0]
    rate_diff = diffusion[0][None]
    rate_flow = transport[0][None]
    variable_count = moved.shape[0]
    ncells = moved.shape[-1]
    nsteps = SUBSTEPS
    for step in range(nsteps):
        padded = padded_2(moved, (("blk", 2),), 1)
        moved = advance_inner(padded, rate_diff, rate_flow)
    column = moved + jnp.einsum("ij,vjc->vic", mixing[0], moved, precision=lax.Precision.HIGHEST)
    surface = column[:, 0, :]
    column_index_list = src_col[0, 0]
    block_count = column_index_list.shape[0]
    slot_count = column_index_list.shape[1]
    group_size = 8
    group_count = block_count // group_size
    cell_iota = jnp.arange(ncells, dtype=jnp.int32)
    surface_pieces = split_pieces(surface)

    def pick_group(index_group):
        selector = (cell_iota[:, None] == index_group[None, :]).astype(jnp.bfloat16)
        total = jnp.dot(surface_pieces[0], selector, preferred_element_type=jnp.float32)
        total = total + jnp.dot(surface_pieces[1], selector, preferred_element_type=jnp.float32)
        return total + jnp.dot(surface_pieces[2], selector, preferred_element_type=jnp.float32)

    picked_groups = lax.map(
        pick_group, column_index_list.reshape(group_count, group_size * slot_count)
    )
    picked = jnp.transpose(
        picked_groups.reshape(group_count, variable_count, group_size, slot_count), (0, 2, 1, 3)
    ).reshape(block_count, variable_count, slot_count)
    active_mask = jnp.arange(slot_count, dtype=jnp.int32)[None, :] < counts[0, 0][:, None]
    outgoing = jnp.where(
        active_mask[:, None, :], weights[0, 0][:, None, :] * picked, jnp.float32(0.0)
    )
    received_rows = lax.all_to_all(outgoing, "blk", split_axis=0, concat_axis=0, tiled=True)
    received_rows = partner(received_rows, "sec", 0)
    value_groups = jnp.transpose(
        received_rows.reshape(group_count, group_size, variable_count, slot_count), (0, 2, 1, 3)
    ).reshape(group_count, variable_count, group_size * slot_count)
    row_groups = recv_rows[0, 0].reshape(group_count, group_size * slot_count)

    def add_group(total, item):
        group_values, group_rows = item
        selector = (group_rows[:, None] == cell_iota[None, :]).astype(jnp.bfloat16)
        return (total + product_sum(group_values, selector), None)

    incoming, unused = lax.scan(
        add_group, jnp.zeros((variable_count, ncells), jnp.float32), (value_groups, row_groups)
    )
    top = surface + 0.5 * (incoming - surface)
    new_state = column.at[:, 0, :].set(top)
    return (new_state[None], incoming[None])


def solution(mesh):
    placed = (
        P("sec", None, None, "blk"),
        P("sec", None, "blk"),
        P("sec", None, "blk"),
        P("sec", None, None),
        P("sec", "blk", None, None),
        P("sec", "blk", None, None),
        P("sec", "blk", None),
        P("sec", "blk", None, None),
    )
    return jax.shard_map(
        body,
        mesh=mesh,
        in_specs=placed,
        out_specs=(P("sec", None, None, "blk"), P("sec", None, "blk")),
        check_vma=False,
    )
```

profile of v0, /device:TPU:1, one launch (start us, length us, event | category | flops | bytes accessed | tf_op | source)
XLA Modules:
  0.0 85.8 jit_solution(456134422508276319)
XLA Ops:
  0.6 0.0 copy-start
  0.7 1.6 %fusion.48 = (f32[32,40,1]{2,1,0:T(8,128)S(1)}, f32[32,40,1]{2,1,0:T(8,128)S(1)}) fusion(f32[32,40,1024]{2,1,0:T(8,128)} %bitcast.97), kind=kLoop, calls=%fused_computation.66 | loop fusion | bytes 20480 | tf_op jit(solution)/shard_map/slice | solution.py:14
  2.2 0.3 copy.15
  2.5 2.1 %collective-permute-start = (f32[32,40,1]{1,0,2:T(8,128)S(1)}, f32[32,40,1]{1,0,2:T(8,128)S(1)}, u32[]{:S(2)}, u32[]{:S(2)}) collective-permute-start(f32[32,40,1]{1,0,2:T(8,128)S(1)} %copy.15), channel_id=1, source_target_pairs={{0,1},{1,2},{2,3},{3,4},{4,5},{5,6},{6,7},{7,8},{8,9},{9,10},{10,1... | collective-permute-start | bytes 15368 | tf_op jit(solution)/shard_map/ppermute | solution.py:16
  4.6 0.3 copy.17
  4.9 4.1 %collective-permute-start.1 = (f32[32,40,1]{1,0,2:T(8,128)S(1)}, f32[32,40,1]{1,0,2:T(8,128)S(1)}, u32[]{:S(2)}, u32[]{:S(2)}) collective-permute-start(f32[32,40,1]{1,0,2:T(8,128)S(1)} %copy.17), channel_id=1, source_target_pairs={{1,0},{2,1},{3,2},{4,3},{5,4},{6,5},{7,6},{8,7},{9,8},{10,9},{11,1... | collective-permute-start | bytes 15368 | tf_op jit(solution)/shard_map/ppermute | solution.py:17
  8.9 0.8 collective-permute-done
  9.7 0.3 copy.16
  10.0 0.3 copy.18
  10.4 0.0 copy-start.9
  10.4 0.0 copy-start.6
  10.4 9.4 %fusion.35 = f32[32,40,1024]{2,1,0:T(8,128)S(1)} fusion(f32[32,40,1024]{2,1,0:T(8,128)} %bitcast.98, f32[32,40,1]{2,1,0:T(8,128)S(1)} %copy.18, f32[32,40,1]{2,1,0:T(8,128)S(1)} %copy.16, f32[40,1024]{1,0:T(8,128)S(1)} %bitcast.106, f32[40,1024]{1,0:T(8,128)S(1)} %bitcast.108), kind=kLoop, calls=%fused_computation.43 | loop fusion | flops 13107200 | bytes 10823680 | tf_op jit(solution)/shard_map/add | solution.py:30
  19.8 0.0 copy-start.1
  19.8 2.3 %copy-done.1 = f32[32,40,1024]{2,1,0:T(8,128)} copy-done((f32[32,40,1024]{2,1,0:T(8,128)}, f32[32,40,1024]{2,1,0:T(8,128)S(1)}, u32[]{:S(2)}) %copy-start.1) | copy-done | bytes 5242904
  22.1 0.2 fusion.47
  22.4 0.3 copy.19
  22.7 0.1 collective-permute-start.2
  22.7 0.3 copy.21
  23.0 5.1 %collective-permute-start.3 = (f32[32,40,1]{1,0,2:T(8,128)S(1)}, f32[32,40,1]{1,0,2:T(8,128)S(1)}, u32[]{:S(2)}, u32[]{:S(2)}) collective-permute-start(f32[32,40,1]{1,0,2:T(8,128)S(1)} %copy.21), channel_id=1, source_target_pairs={{1,0},{2,1},{3,2},{4,3},{5,4},{6,5},{7,6},{8,7},{9,8},{10,9},{11,1... | collective-permute-start | bytes 15368 | tf_op jit(solution)/shard_map/ppermute | solution.py:17
  28.1 0.1 iota_compare_fusion.22
  28.2 0.7 collective-permute-done.2
  28.9 0.3 copy.20
  29.2 0.3 copy.22
  29.5 20.3 %bitcast_add_fusion = f32[32,40,1024]{2,1,0:T(8,128)S(1)} fusion(f32[32,40,1024]{2,1,0:T(8,128)} %copy-done.1, f32[40,1024]{1,0:T(8,128)S(1)} %bitcast.107, f32[32,40,1]{2,1,0:T(8,128)S(1)} %copy.22, f32[32,40,1]{2,1,0:T(8,128)S(1)} %copy.20, f32[40,1024]{1,0:T(8,128)S(1)} %bitcast.109, f32[1,40,40]{2,1,0:T(8,128)S(1)} %copy-done), kind=kOutput, calls=%fused_computation.48 | convolution fusion | flops 656670720 | bytes 10830080 | tf_op jit(solution)/shard_map/ij,vjc->vic/dot_general | solution.py:60
  49.9 0.0 copy-start.8
  49.9 0.1 slice.64
  50.1 2.2 %copy-done.8 = f32[32,40,1024]{2,1,0:T(8,128)} copy-done((f32[32,40,1024]{2,1,0:T(8,128)}, f32[32,40,1024]{2,1,0:T(8,128)S(1)}, u32[]{:S(2)}) %copy-start.8) | copy-done | bytes 5242904
  52.2 4.6 %while.23 = (s32[]{:T(128)}, f32[2,32,1024]{2,1,0:T(8,128)S(1)}, s32[2,1024]{1,0:T(2,128)S(1)}, bf16[32,1024]{1,0:T(8,128)(2,1)S(1)}, bf16[32,1024]{1,0:T(8,128)...) while((s32[]{:T(128)}, f32[2,32,1024]{2,1,0:T(8,128)S(1)}, s32[2,1024]{1,0:T(2,128)S(1)}, ...), condition=%wide.region_1.2_spmd.clone, body=%wide.region_0.1_spmd.clone.sunk | while | flops 204537856 | bytes 872533 | solution.py:76
  52.3 0.8 fusion.69
  53.0 0.8 fusion.70
  53.8 0.8 fusion.71
  54.6 0.8 fusion.69
  55.3 0.8 fusion.70
  56.1 0.8 fusion.71
  57.0 0.1 copy.23
  57.1 13.8 %all_to_all.5 = f32[16,32,128]{2,1,0:T(8,128)S(1)} all-to-all(f32[16,32,128]{2,1,0:T(8,128)S(1)} %fusion.40), channel_id=1, replica_groups=mesh['sec'=2,'blk'=16] {'blk'}, dimensions={0} | all-to-all | bytes 524288 | tf_op jit(solution)/shard_map/all_to_all | solution.py:86
  70.8 4.3 %collective-permute-start.4 = (f32[16,32,128]{2,1,0:T(8,128)S(1)}, f32[16,32,128]{2,1,0:T(8,128)S(1)}, u32[]{:S(2)}, u32[]{:S(2)}) collective-permute-start(f32[16,32,128]{2,1,0:T(8,128)S(1)} %all_to_all.5), channel_id=1, source_target_pairs={{0,16},{16,0},{1,17},{17,1},{2,18},{18,2},{3,19},{19,3},{4,20},{20... | collective-permute-start | bytes 786440 | tf_op jit(solution)/shard_map/ppermute | solution.py:23
  75.1 1.1 %collective-permute-done.4 = f32[16,32,128]{2,1,0:T(8,128)S(1)} collective-permute-done((f32[16,32,128]{2,1,0:T(8,128)S(1)}, f32[16,32,128]{2,1,0:T(8,128)S(1)}, u32[]{:S(2)}, u32[]{:S(2)}) %collective-permute-start.4) | collective-permute-done | bytes 262176 | tf_op jit(solution)/shard_map/ppermute | solution.py:23
  76.3 5.7 %while.24 = (s32[]{:T(128)}, f32[32,1024]{1,0:T(8,128)S(1)}, f32[2,32,1024]{2,1,0:T(8,128)S(1)}, s32[2,1024]{1,0:T(2,128)S(1)}, s32[]{:T(128)}, /*index=5*/s32[]{:T(128)}) while((s32[]{:T(128)}, f32[32,1024]{1,0:T(8,128)S(1)}, f32[2,32,1024]{2,1,0:T(8,128)S(1)}, s32[2,1024]{1,0:T(2,128)S(1)}, s32[]{:T(128)}, ...), condition=%wide.region_3.4_spmd.clone, body=%wide.region_2.3_spmd.clone.sunk | while | flops 204865536 | bytes 1593439 | solution.py:98
  76.3 0.9 %fusion.75 = f32[32,1024]{1,0:T(8,128)S(1)} fusion(s32[1024]{0:T(1024)S(1)} %bitcast.111, bf16[32,1024]{1,0:T(8,128)(2,1)S(1)} %fusion.74, bf16[32,1024]{1,0:T(8,128)(2,1)S(1)} %bitcast_convert_fusion.3, f32[2,32,1024]{2,1,0:T(8,128)S(1)} %get-tuple-element.232, s32[]{:T(128)} %get-tuple-element.224), kind=kOutput, calls=%fused_computation.15.clone.1 | convolution fusion | flops 68321280 | bytes 397316 | tf_op jit(solution)/shard_map/while/body/eval_jaxpr/dot_general | solution.py:47
  77.3 0.9 %fusion.76 = f32[32,1024]{1,0:T(8,128)S(1)} fusion(bf16[32,1024]{1,0:T(8,128)(2,1)S(1)} %fusion.74, s32[1024]{0:T(1024)S(1)} %bitcast.112), kind=kOutput, calls=%fused_computation.16.clone.1 | convolution fusion | flops 68157440 | bytes 200704 | tf_op jit(solution)/shard_map/while/body/eval_jaxpr/dot_general | solution.py:46
  78.2 0.9 %fusion.77 = f32[32,1024]{1,0:T(8,128)S(1)} fusion(f32[32,1024]{1,0:T(8,128)S(1)} %fusion.75, f32[32,1024]{1,0:T(8,128)S(1)} %fusion.76, bf16[32,1024]{1,0:T(8,128)(2,1)S(1)} %bitcast_convert_fusion.3, s32[1024]{0:T(1024)S(1)} %bitcast.113, f32[32,1024]{1,0:T(8,128)S(1)} %get-tuple-element.225, pred[]{:T(512)S(6)} %compare.9), kind=kOutput, calls=%fused_computation.23.clone.1 | convolution fusion | flops 68288512 | bytes 593921 | tf_op jit(solution)/shard_map/while/body/eval_jaxpr/dot_general | solution.py:45
  79.2 0.9 %fusion.75 = f32[32,1024]{1,0:T(8,128)S(1)} fusion(s32[1024]{0:T(1024)S(1)} %bitcast.111, bf16[32,1024]{1,0:T(8,128)(2,1)S(1)} %fusion.74, bf16[32,1024]{1,0:T(8,128)(2,1)S(1)} %bitcast_convert_fusion.3, f32[2,32,1024]{2,1,0:T(8,128)S(1)} %get-tuple-element.232, s32[]{:T(128)} %get-tuple-element.224), kind=kOutput, calls=%fused_computation.15.clone.1 | convolution fusion | flops 68321280 | bytes 397316 | tf_op jit(solution)/shard_map/while/body/eval_jaxpr/dot_general | solution.py:47
  80.2 0.9 %fusion.76 = f32[32,1024]{1,0:T(8,128)S(1)} fusion(bf16[32,1024]{1,0:T(8,128)(2,1)S(1)} %fusion.74, s32[1024]{0:T(1024)S(1)} %bitcast.112), kind=kOutput, calls=%fused_computation.16.clone.1 | convolution fusion | flops 68157440 | bytes 200704 | tf_op jit(solution)/shard_map/while/body/eval_jaxpr/dot_general | solution.py:46
  81.1 0.9 %fusion.77 = f32[32,1024]{1,0:T(8,128)S(1)} fusion(f32[32,1024]{1,0:T(8,128)S(1)} %fusion.75, f32[32,1024]{1,0:T(8,128)S(1)} %fusion.76, bf16[32,1024]{1,0:T(8,128)(2,1)S(1)} %bitcast_convert_fusion.3, s32[1024]{0:T(1024)S(1)} %bitcast.113, f32[32,1024]{1,0:T(8,128)S(1)} %get-tuple-element.225, pred[]{:T(512)S(6)} %compare.9), kind=kOutput, calls=%fused_computation.23.clone.1 | convolution fusion | flops 68288512 | bytes 593921 | tf_op jit(solution)/shard_map/while/body/eval_jaxpr/dot_general | solution.py:45
  82.0 0.0 copy-start.4
  82.1 0.1 copy.25
  82.2 3.6 %scatter.4 = f32[1,32,40,1024]{3,2,1,0:T(8,128)} dynamic-update-slice(f32[1,32,40,1024]{3,2,1,0:T(8,128)} %bitcast.118, f32[1,32,1,1024]{3,2,1,0:T(1,128)S(1)} %copy.25, s32[]{:T(128)} %constant.51.clone.1, s32[]{:T(128)} %constant.51.clone.1, s32[]{:T(128)} %constant.51.clone.1, s32[]{:T(128)} %constant.51.clone.1) | dynamic-update-slice | bytes 262148 | tf_op jit(solution)/shard_map/scatter | solution.py:102
  (34 shorter events, 0.4 us)
Async XLA Ops:
  0.6 28.9 %copy-start = (f32[1,40,40]{2,1,0:T(8,128)S(1)}, f32[1,40,40]{2,1,0:T(8,128)}, u32[]{:S(2)}) copy-start(f32[1,40,40]{2,1,0:T(8,128)} %param.17) | copy-start | bytes 19204
  0.6 9.7 %copy-start.3 = (f32[1,40,1024]{2,1,0:T(8,128)S(1)}, f32[1,40,1024]{2,1,0:T(8,128)}, u32[]{:S(2)}) copy-start(f32[1,40,1024]{2,1,0:T(8,128)} %param.15) | copy-start | bytes 491524
  0.7 9.7 %copy-start.2 = (f32[1,40,1024]{2,1,0:T(8,128)S(1)}, f32[1,40,1024]{2,1,0:T(8,128)}, u32[]{:S(2)}) copy-start(f32[1,40,1024]{2,1,0:T(8,128)} %param.16) | copy-start | bytes 491524
  2.5 7.2 %collective-permute-start = (f32[32,40,1]{1,0,2:T(8,128)S(1)}, f32[32,40,1]{1,0,2:T(8,128)S(1)}, u32[]{:S(2)}, u32[]{:S(2)}) collective-permute-start(f32[32,40,1]{1,0,2:T(8,128)S(1)} %copy.15), channel_id=1, source_target_pairs={{0,1},{1,2},{2,3},{3,4},{4,5},{5,6},{6,7},{7,8},{8,9},{9,10},{10,1... | collective-permute-start | bytes 15368 | tf_op jit(solution)/shard_map/ppermute | solution.py:16
  4.9 5.2 %collective-permute-start.1 = (f32[32,40,1]{1,0,2:T(8,128)S(1)}, f32[32,40,1]{1,0,2:T(8,128)S(1)}, u32[]{:S(2)}, u32[]{:S(2)}) collective-permute-start(f32[32,40,1]{1,0,2:T(8,128)S(1)} %copy.17), channel_id=1, source_target_pairs={{1,0},{2,1},{3,2},{4,3},{5,4},{6,5},{7,6},{8,7},{9,8},{10,9},{11,1... | collective-permute-start | bytes 15368 | tf_op jit(solution)/shard_map/ppermute | solution.py:17
  10.4 17.7 %copy-start.9 = (s32[1,1,16]{2,1,0:T(1,128)S(1)}, s32[1,1,16]{2,1,0:T(1,128)}, u32[]{:S(2)}) copy-start(s32[1,1,16]{2,1,0:T(1,128)} %param.20) | copy-start | bytes 196
  10.4 17.8 %copy-start.6 = (s32[1,1,16,128]{3,2,1,0:T(8,128)S(1)}, s32[1,1,16,128]{3,2,1,0:T(8,128)}, u32[]{:S(2)}) copy-start(s32[1,1,16,128]{3,2,1,0:T(8,128)} %param.18) | copy-start | bytes 24580
  19.8 2.4 %copy-start.1 = (f32[32,40,1024]{2,1,0:T(8,128)}, f32[32,40,1024]{2,1,0:T(8,128)S(1)}, u32[]{:S(2)}) copy-start(f32[32,40,1024]{2,1,0:T(8,128)S(1)} %fusion.35) | copy-start | bytes 15728644
  22.7 6.3 %collective-permute-start.2 = (f32[32,40,1]{1,0,2:T(8,128)S(1)}, f32[32,40,1]{1,0,2:T(8,128)S(1)}, u32[]{:S(2)}, u32[]{:S(2)}) collective-permute-start(f32[32,40,1]{1,0,2:T(8,128)S(1)} %copy.19), channel_id=1, source_target_pairs={{0,1},{1,2},{2,3},{3,4},{4,5},{5,6},{6,7},{7,8},{8,9},{9,10},{10,1... | collective-permute-start | bytes 15368 | tf_op jit(solution)/shard_map/ppermute | solution.py:16
  23.0 6.2 %collective-permute-start.3 = (f32[32,40,1]{1,0,2:T(8,128)S(1)}, f32[32,40,1]{1,0,2:T(8,128)S(1)}, u32[]{:S(2)}, u32[]{:S(2)}) collective-permute-start(f32[32,40,1]{1,0,2:T(8,128)S(1)} %copy.21), channel_id=1, source_target_pairs={{1,0},{2,1},{3,2},{4,3},{5,4},{6,5},{7,6},{8,7},{9,8},{10,9},{11,1... | collective-permute-start | bytes 15368 | tf_op jit(solution)/shard_map/ppermute | solution.py:17
  49.9 2.4 %copy-start.8 = (f32[32,40,1024]{2,1,0:T(8,128)}, f32[32,40,1024]{2,1,0:T(8,128)S(1)}, u32[]{:S(2)}) copy-start(f32[32,40,1024]{2,1,0:T(8,128)S(1)} %bitcast_add_fusion) | copy-start | bytes 15728644
  52.2 4.8 %copy-start.5 = (f32[1,1,16,128]{3,2,1,0:T(8,128)S(1)}, f32[1,1,16,128]{3,2,1,0:T(8,128)}, u32[]{:S(2)}) copy-start(f32[1,1,16,128]{3,2,1,0:T(8,128)} %param.19) | copy-start | bytes 24580
  52.2 22.8 %copy-start.7 = (s32[1,1,16,128]{3,2,1,0:T(8,128)S(1)}, s32[1,1,16,128]{3,2,1,0:T(8,128)}, u32[]{:S(2)}) copy-start(s32[1,1,16,128]{3,2,1,0:T(8,128)} %param.21) | copy-start | bytes 24580
  70.8 5.4 %collective-permute-start.4 = (f32[16,32,128]{2,1,0:T(8,128)S(1)}, f32[16,32,128]{2,1,0:T(8,128)S(1)}, u32[]{:S(2)}, u32[]{:S(2)}) collective-permute-start(f32[16,32,128]{2,1,0:T(8,128)S(1)} %all_to_all.5), channel_id=1, source_target_pairs={{0,16},{16,0},{1,17},{17,1},{2,18},{18,2},{3,19},{19,3},{4,20},{20... | collective-permute-start | bytes 786440 | tf_op jit(solution)/shard_map/ppermute | solution.py:23
  82.0 3.8 %copy-start.4 = (f32[32,1024]{1,0:T(8,128)}, f32[32,1024]{1,0:T(8,128)S(1)}, u32[]{:S(2)}) copy-start(f32[32,1024]{1,0:T(8,128)S(1)} %get-tuple-element.79) | copy-start | bytes 393220
where the time goes:
time: 86.4 us; the launch traced here: 85.8 us
  matrix products  30.4 us (35%)
  starting transfers between devices  15.6 us (18%)
  blocking collectives  13.8 us (16%)
  local copies, waits for them, and re-layouts  12.7 us (15%)
  other arithmetic  9.63 us (11%)
  waiting for transfers between devices  2.66 us (3%)
    dot_general x1, matrix products, body(): jnp.einsum('ij,vjc->vic', mixing[0], moved, precision=lax.Precision.HIGHEST)  20.3 us
    all_to_all x1, blocking collectives, body(): lax.all_to_all(outgoing, 'blk', split_axis=0, concat_axis=0, tiled=True)  13.8 us
    add x1, other arithmetic, advance_inner(): middle + rate_diff * (left - 2.0 * middle + right)  9.39 us
    ppermute x2, starting transfers between devices, padded_2(): after = lax.ppermute(leading, axis, down)  9.18 us
    unnamed x22, local copies, waits for them, and re-layouts  4.64 us
    ppermute x1, starting transfers between devices, partner(): lax.ppermute(x, axis, [(i, i ^ 1 << apart) for i in range(lax.axis_size(a...  4.26 us
    scatter x1, local copies, waits for them, and re-layouts, body(): new_state = column.at[:, 0, :].set(top)  3.63 us
    slice x4, local copies, waits for them, and re-layouts, padded_2(): last = lax.slice_in_dim(x, length - width, length, axis=dim)  2.35 us
  transfers between devices with their start and end apart: 5, of which 3 were waited for; matrix products, arithmetic and copies ran while one was open for 1% of the time, Pallas kernels for 0%

commit v1 on v0

v1 whole, which is shorter than its diff:
```python
import functools

import jax
import jax.numpy as jnp
from jax import lax
from jax.experimental import pallas as pl
from jax.experimental.pallas import tpu as pltpu
from jax.sharding import PartitionSpec as P

MESH = pl.DeviceIdType.MESH
F32 = jnp.float32
BF16 = jnp.bfloat16
GROUP = 2
CHUNKS = 4
LANES = 128
SELECTOR_BYTES = 8 << 20


def lanes_of(shape):
    return lax.broadcasted_iota(jnp.int32, shape, len(shape) - 1)


def rows_of(shape):
    return lax.broadcasted_iota(jnp.int32, shape, len(shape) - 2)


def column_of(row, count):
    shape = (count, row.shape[1])
    spread = jnp.where(lanes_of(shape) == rows_of(shape), jnp.broadcast_to(row, shape), 0.0)
    return jnp.sum(spread, axis=1, keepdims=True)


def pieces_of(values):
    high = values.astype(BF16)
    low = (values - high.astype(F32)).astype(BF16)
    return jnp.concatenate([high, low], axis=0)


def kernel(
    nblocks, prebuilt,
    state, diffusion, transport, mixing, src_col, weights, counts, recv_rows,
    out, incoming,
    u, dif, tra, mix, src, wgt, cnt, rec,
    rate_a, rate_b, rate_d, edge_l, edge_r, msg_l, msg_r, from_l, from_r,
    surf, sendbuf, recvbuf, total, picker, placer,
    chunk_sem, small_sem, halo_send, halo_recv, send_sem, recv_sem,
):
    nvar, nlev, ncell = u.shape
    nslot = src.shape[1]
    ngroup = nblocks // GROUP
    sec = lax.axis_index("sec")
    blk = lax.axis_index("blk")
    other = 1 - sec
    left = lax.rem(blk + nblocks - 1, nblocks)
    right = lax.rem(blk + 1, nblocks)
    barrier = pltpu.get_barrier_semaphore()

    @pl.loop(0, nblocks)
    def greet(k):
        pl.semaphore_signal(barrier, inc=1, device_id=(other, lax.rem(blk + k, nblocks)), device_id_type=MESH)

    for side in (left, right):
        pl.semaphore_signal(barrier, inc=1, device_id=(sec, side), device_id_type=MESH)

    small = [
        pltpu.make_async_copy(source, target, small_sem.at[i])
        for i, (source, target) in enumerate(
            (
                (src_col.at[0, 0], src),
                (diffusion.at[0], dif),
                (transport.at[0], tra),
                (mixing.at[0], mix),
                (weights.at[0, 0], wgt),
                (counts.at[0], cnt),
                (recv_rows.at[0, 0], rec),
            )
        )
    ]
    for copy in small:
        copy.start()
    per_chunk = nvar // CHUNKS
    chunks = [
        pltpu.make_async_copy(
            state.at[0, pl.ds(i * per_chunk, per_chunk)],
            u.at[pl.ds(i * per_chunk, per_chunk)],
            chunk_sem.at[i],
        )
        for i in range(CHUNKS)
    ]
    for copy in chunks:
        copy.start()
    for copy in small:
        copy.wait()

    def selector(index_ref, base):
        parts = []
        for g in range(GROUP):
            row = index_ref[pl.ds(base + g, 1), :]
            cells = rows_of((ncell, nslot))
            parts.append(jnp.where(cells == jnp.broadcast_to(row, (ncell, nslot)), 1.0, 0.0).astype(BF16))
        return jnp.concatenate(parts, axis=1)

    cell = lanes_of((nlev, ncell))
    d_all = dif[...]
    b_all = d_all + tra[...]
    rate_a[...] = 1.0 - d_all - b_all
    rate_b[...] = jnp.where(cell == 0, 0.0, b_all)
    rate_d[...] = jnp.where(cell == ncell - 1, 0.0, d_all)
    d_first, d_last = dif[:, :LANES], dif[:, ncell - LANES :]
    b_first = d_first + tra[:, :LANES]
    b_last = d_last + tra[:, ncell - LANES :]
    a_first, a_last = 1.0 - d_first - b_first, 1.0 - d_last - b_last
    a0, b0, b1, d0 = a_first[:, 0:1], b_first[:, 0:1], b_first[:, 1:2], d_first[:, 0:1]
    an, bn = a_last[:, LANES - 1 :], b_last[:, LANES - 1 :]
    dn, dm = d_last[:, LANES - 1 :], d_last[:, LANES - 2 : LANES - 1]

    if prebuilt:

        @pl.loop(0, ngroup)
        def build_picker(g):
            picker[g] = selector(src, g * GROUP)

    live = lanes_of(wgt.shape).astype(F32) < column_of(cnt[...].astype(F32), nblocks)
    wgt[...] = jnp.where(live, wgt[...], 0.0)

    lane = lanes_of((nlev, LANES))
    even = lax.rem(lane, 2) == 0
    edge_l[...] = jnp.zeros_like(edge_l)
    edge_r[...] = jnp.zeros_like(edge_r)
    for i in range(CHUNKS):
        chunks[i].wait()

        @pl.loop(i * per_chunk, (i + 1) * per_chunk)
        def pack(v):
            mine = lax.div(lane, 2) == v
            first = pltpu.roll(u[v, :, 0:LANES], 2 * v, 1)
            last = pltpu.roll(u[v, :, ncell - LANES : ncell], 2 * v + 2, 1)
            edge_l[...] = jnp.where(mine, first, edge_l[...])
            edge_r[...] = jnp.where(mine, last, edge_r[...])

    el, er = edge_l[...], edge_r[...]
    after = lambda x: pltpu.roll(x, LANES - 1, 1)
    before = lambda x: pltpu.roll(x, 1, 1)
    is_rate = lane == 2 * nvar
    msg_r[...] = jnp.where(is_rate, dn, jnp.where(even, after(er), an * er + bn * before(er)))
    msg_l[...] = jnp.where(is_rate, b0, jnp.where(even, el, before(a0 * el + d0 * after(el))))

    pl.semaphore_wait(barrier, nblocks + 2)
    to_right = pltpu.make_async_remote_copy(
        src_ref=msg_r, dst_ref=from_l, send_sem=halo_send.at[0], recv_sem=halo_recv.at[0],
        device_id=(sec, right), device_id_type=MESH,
    )
    to_left = pltpu.make_async_remote_copy(
        src_ref=msg_l, dst_ref=from_r, send_sem=halo_send.at[1], recv_sem=halo_recv.at[1],
        device_id=(sec, left), device_id_type=MESH,
    )
    to_right.start()
    to_left.start()

    top_mix = column_of(mix[0:1, :], nlev)
    top_mix = top_mix + jnp.where(rows_of((nlev, 1)) == 0, 1.0, 0.0)

    @pl.loop(0, nvar)
    def transport_substeps(v):
        acc = jnp.zeros((8, ncell), F32)
        for g in range(nlev // 8):
            span = slice(8 * g, 8 * g + 8)
            a, b, d = rate_a[span, :], rate_b[span, :], rate_d[span, :]
            x = u[v, span, :]
            for step in range(2):
                x = a * x + b * pltpu.roll(x, 1, 1) + d * pltpu.roll(x, ncell - 1, 1)
            u[v, span, :] = x
            acc = acc + top_mix[span, :] * x
        surf[pl.ds(v, 1), :] = jnp.sum(acc, axis=0, keepdims=True)

    to_right.wait()
    to_left.wait()

    fl, fr = from_l[...], from_r[...]
    rate_l, rate_r = fl[:, 2 * nvar : 2 * nvar + 1], fr[:, 2 * nvar : 2 * nvar + 1]
    add_l = jnp.where(
        even, a0 * b0 * fl + b0 * (after(fl) + rate_l * el), b1 * b0 * before(fl)
    )
    add_r = jnp.where(
        even, dm * dn * fr, an * dn * before(fr) + dn * (fr + rate_r * er)
    )
    edge_l[...] = add_l
    edge_r[...] = add_r
    wide = (nvar, LANES)
    wide_lane, wide_row = lanes_of(wide), rows_of(wide)
    for add, start, low in ((add_l, 0, 0), (add_r, ncell - LANES, LANES - 2)):
        row = jnp.broadcast_to(jnp.sum(top_mix * add, axis=0, keepdims=True), wide)
        fix = jnp.zeros(wide, F32)
        for k in range(2):
            value = jnp.sum(jnp.where(wide_lane == 2 * wide_row + k, row, 0.0), axis=1, keepdims=True)
            fix = fix + jnp.where(wide_lane == low + k, value, 0.0)
        surf[:, start : start + LANES] = surf[:, start : start + LANES] + fix

    my_group = lax.div(blk, GROUP)
    surf_pieces = pieces_of(surf[...])

    def contribution(d):
        return pltpu.make_async_remote_copy(
            src_ref=sendbuf.at[d], dst_ref=recvbuf.at[blk],
            send_sem=send_sem.at[d], recv_sem=recv_sem.at[blk],
            device_id=(other, d), device_id_type=MESH,
        )

    @pl.loop(0, ngroup)
    def pick(k):
        group = lax.rem(my_group + k, ngroup)
        chosen = picker[group] if prebuilt else selector(src, group * GROUP)
        both = jnp.dot(surf_pieces, chosen, preferred_element_type=F32)
        values = both[:nvar] + both[nvar:]
        for g in range(GROUP):
            d = group * GROUP + g
            sendbuf[d] = values[:, g * nslot : (g + 1) * nslot] * wgt[pl.ds(d, 1), :]
            contribution(d).start()

    m_high = mix[...].astype(BF16).astype(F32)
    m_low = mix[...] - m_high
    m_row = jnp.concatenate([m_high, m_low, m_high], axis=1)
    m_none = jnp.zeros_like(m_row)
    m_pair = jnp.concatenate(
        [jnp.concatenate([m_row, m_none], axis=1), jnp.concatenate([m_none, m_row], axis=1)], axis=0
    ).astype(BF16)

    @pl.loop(0, nvar // 2)
    def mix_pair(pair):
        stack, moved = [], []
        for i in range(2):
            v = 2 * pair + i
            first = u[v, :, 0:LANES] + jnp.where(lane < 2, pltpu.roll(edge_l[...], LANES - 2 * v, 1), 0.0)
            last = u[v, :, ncell - LANES : ncell] + jnp.where(
                lane >= LANES - 2, pltpu.roll(edge_r[...], LANES - 2 - 2 * v, 1), 0.0
            )
            x = jnp.concatenate([first, u[v, :, LANES : ncell - LANES], last], axis=1)
            high = x.astype(BF16).astype(F32)
            stack += [high, high, x - high]
            moved.append(x)
        mixed = jnp.dot(
            m_pair, jnp.concatenate(stack, axis=0).astype(BF16), preferred_element_type=F32
        )
        for i in range(2):
            out[0, 2 * pair + i] = moved[i] + mixed[i * nlev : (i + 1) * nlev]

    if prebuilt:

        @pl.loop(0, ngroup)
        def build_placer(g):
            placer[g] = selector(rec, g * GROUP)

    total[...] = jnp.zeros_like(total)

    @pl.loop(0, ngroup)
    def place(k):
        group = lax.rem(my_group - k + ngroup, ngroup)
        chosen = placer[group] if prebuilt else selector(rec, group * GROUP)
        values = []
        for g in range(GROUP):
            b = group * GROUP + g
            pltpu.make_async_remote_copy(
                src_ref=sendbuf.at[b], dst_ref=recvbuf.at[b],
                send_sem=send_sem.at[b], recv_sem=recv_sem.at[b],
                device_id=(other, b), device_id_type=MESH,
            ).wait_recv()
            values.append(recvbuf[b])
        total[...] += lax.dot_general(
            pieces_of(jnp.concatenate(values, axis=1)), chosen, (((1,), (1,)), ((), ())),
            preferred_element_type=F32,
        )

    arrived = total[:nvar] + total[nvar:]
    incoming[0] = arrived
    surface = surf[...]
    out[0, :, 0, :] = surface + 0.5 * (arrived - surface)

    @pl.loop(0, nblocks)
    def sent(d):
        contribution(d).wait_send()


def body(state, diffusion, transport, mixing, src_col, weights, counts, recv_rows):
    _, nvar, nlev, ncell = state.shape
    nblocks, nslot = src_col.shape[2:]
    ngroup = nblocks // GROUP
    prebuilt = nblocks * nslot * ncell * 2 <= SELECTOR_BYTES
    chosen = (ngroup, ncell, GROUP * nslot) if prebuilt else (1, 16, LANES)
    edge = pltpu.VMEM((nlev, LANES), F32)
    rate = pltpu.VMEM((nlev, ncell), F32)
    dma = pltpu.SemaphoreType.DMA
    return pl.pallas_call(
        functools.partial(kernel, nblocks, prebuilt),
        out_shape=(
            jax.ShapeDtypeStruct(state.shape, F32),
            jax.ShapeDtypeStruct((1, nvar, ncell), F32),
        ),
        in_specs=[pl.BlockSpec(memory_space=pl.ANY)] * 8,
        out_specs=[pl.BlockSpec(memory_space=pltpu.VMEM)] * 2,
        scratch_shapes=[
            pltpu.VMEM((nvar, nlev, ncell), F32),
            rate, rate,
            pltpu.VMEM((nlev, nlev), F32),
            pltpu.VMEM((nblocks, nslot), jnp.int32),
            pltpu.VMEM((nblocks, nslot), F32),
            pltpu.VMEM((1, nblocks), jnp.int32),
            pltpu.VMEM((nblocks, nslot), jnp.int32),
            rate, rate, rate,
            edge, edge, edge, edge, edge, edge,
            pltpu.VMEM((nvar, ncell), F32),
            pltpu.VMEM((nblocks, nvar, nslot), F32),
            pltpu.VMEM((nblocks, nvar, nslot), F32),
            pltpu.VMEM((2 * nvar, ncell), F32),
            pltpu.VMEM(chosen, BF16),
            pltpu.VMEM(chosen, BF16),
            dma((CHUNKS,)), dma((7,)), dma((2,)), dma((2,)),
            dma((nblocks,)), dma((nblocks,)),
        ],
        compiler_params=pltpu.CompilerParams(
            collective_id=0, has_side_effects=True, vmem_limit_bytes=40 << 20
        ),
        cost_estimate=pl.CostEstimate(
            flops=10**9, bytes_accessed=11 * 10**6, transcendentals=0
        ),
    )(state, diffusion, transport, mixing, src_col, weights, counts, recv_rows)


def solution(mesh):
    placed = (
        P("sec", None, None, "blk"),
        P("sec", None, "blk"),
        P("sec", None, "blk"),
        P("sec", None, None),
        P("sec", "blk", None, None),
        P("sec", "blk", None, None),
        P("sec", "blk", None),
        P("sec", "blk", None, None),
    )
    return jax.shard_map(
        body,
        mesh=mesh,
        in_specs=placed,
        out_specs=(P("sec", None, None, "blk"), P("sec", None, "blk")),
        check_vma=False,
    )
```

time: 86.4 us -> 39.8 us (0.46)
  matrix products: 30.4 us -> 0 us
  Pallas kernels: 0 us -> 27.6 us
  starting transfers between devices: 15.6 us -> 0 us
  blocking collectives: 13.8 us -> 0 us
  other arithmetic: 9.63 us -> 0 us
  waiting for transfers between devices: 2.66 us -> 0 us
  local copies, waits for them, and re-layouts: 12.7 us -> 10.8 us
    dot_general x13 -> x0, matrix products: 30.4 us -> none  [the longest x1 20.3 us: body(): jnp.einsum('ij,vjc->vic', mixing[0], moved, precision=lax.Precision.HIGHEST)]
    pallas_call x0 -> x1, Pallas kernels: none -> 27.6 us  [body(): pl.pallas_call(functools.partial(kernel, nblocks, prebuilt), out_shape=(j...]
    ppermute x5 -> x0, starting transfers between devices: 15.6 us -> none  [the longest x2 9.18 us: padded_2(): after = lax.ppermute(leading, axis, down)]
    all_to_all x1 -> x0, blocking collectives: 13.8 us -> none  [body(): lax.all_to_all(outgoing, 'blk', split_axis=0, concat_axis=0, tiled=True)]
    add x1 -> x0, other arithmetic: 9.39 us -> none  [advance_inner(): middle + rate_diff * (left - 2.0 * middle + right)]
    unnamed x22 -> x18, local copies, waits for them, and re-layouts: 4.64 us -> 10.8 us
    scatter x1 -> x0, local copies, waits for them, and re-layouts: 3.63 us -> none  [body(): new_state = column.at[:, 0, :].set(top)]
    slice x7 -> x0, local copies, waits for them, and re-layouts: 2.95 us -> none  [the longest x4 2.35 us: padded_2(): last = lax.slice_in_dim(x, length - width, length, axis=dim)]
  transfers between devices with their start and end apart: 5 -> 0, of which waited for: 3 -> 0; matrix products, arithmetic and copies ran while one was open for 1% -> 0% of each run, Pallas kernels for 0% -> 0%
where the time goes in v1:
time: 39.8 us; the launch traced here: 39 us
  Pallas kernels  27.6 us (69%)
  local copies, waits for them, and re-layouts  10.8 us (27%)
  between operations  0.66 us (2%)
    pallas_call x1, Pallas kernels, body(): pl.pallas_call(functools.partial(kernel, nblocks, prebuilt), out_shape=(j...  27.6 us
    unnamed x18, local copies, waits for them, and re-layouts  10.8 us

profile of v1, /device:TPU:1, one launch (start us, length us, event | category | flops | bytes accessed | tf_op | source)
XLA Modules:
  0.0 39.0 jit_solution(13056982986320114928)
XLA Ops:
  0.6 0.0 copy-start
  0.6 2.5 %copy-done = f32[1,32,40,1024]{3,2,1,0:T(8,128)S(1)} copy-done((f32[1,32,40,1024]{3,2,1,0:T(8,128)S(1)}, f32[1,32,40,1024]{3,2,1,0:T(8,128)}, u32[]{:S(2)}) %copy-start) | copy-done | bytes 5242904
  3.1 0.0 copy-start.1
  3.1 0.9 %copy-done.1 = f32[1,40,1024]{2,1,0:T(8,128)S(1)} copy-done((f32[1,40,1024]{2,1,0:T(8,128)S(1)}, f32[1,40,1024]{2,1,0:T(8,128)}, u32[]{:S(2)}) %copy-start.1) | copy-done | bytes 163864
  4.0 0.0 copy-start.2
  4.0 0.9 %copy-done.2 = f32[1,40,1024]{2,1,0:T(8,128)S(1)} copy-done((f32[1,40,1024]{2,1,0:T(8,128)S(1)}, f32[1,40,1024]{2,1,0:T(8,128)}, u32[]{:S(2)}) %copy-start.2) | copy-done | bytes 163864
  5.0 0.0 copy-start.3
  5.0 0.7 %copy-done.3 = f32[1,40,40]{2,1,0:T(8,128)S(1)} copy-done((f32[1,40,40]{2,1,0:T(8,128)S(1)}, f32[1,40,40]{2,1,0:T(8,128)}, u32[]{:S(2)}) %copy-start.3) | copy-done | bytes 6424
  5.7 0.0 copy-start.4
  5.7 0.7 %copy-done.4 = s32[1,1,16,128]{3,2,1,0:T(8,128)S(1)} copy-done((s32[1,1,16,128]{3,2,1,0:T(8,128)S(1)}, s32[1,1,16,128]{3,2,1,0:T(8,128)}, u32[]{:S(2)}) %copy-start.4) | copy-done | bytes 8216
  6.4 0.0 copy-start.5
  6.4 0.7 %copy-done.5 = f32[1,1,16,128]{3,2,1,0:T(8,128)S(1)} copy-done((f32[1,1,16,128]{3,2,1,0:T(8,128)S(1)}, f32[1,1,16,128]{3,2,1,0:T(8,128)}, u32[]{:S(2)}) %copy-start.5) | copy-done | bytes 8216
  7.1 0.0 copy-start.6
  7.1 0.7 %copy-done.6 = s32[1,1,16,128]{3,2,1,0:T(8,128)S(1)} copy-done((s32[1,1,16,128]{3,2,1,0:T(8,128)S(1)}, s32[1,1,16,128]{3,2,1,0:T(8,128)}, u32[]{:S(2)}) %copy-start.6) | copy-done | bytes 8216
  7.8 0.0 copy-start.7
  7.8 0.7 %copy-done.7 = s32[1,1,16]{2,1,0:T(1,128)S(1)} copy-done((s32[1,1,16]{2,1,0:T(1,128)S(1)}, s32[1,1,16]{2,1,0:T(1,128)}, u32[]{:S(2)}) %copy-start.7) | copy-done | bytes 88
  8.4 27.6 %shard_map.95 = (f32[1,32,40,1024]{3,2,1,0:T(8,128)S(1)}, f32[1,32,1024]{2,1,0:T(8,128)S(1)}) custom-call(f32[1,32,40,1024]{3,2,1,0:T(8,128)S(1)} %copy-done, f32[1,40,1024]{2,1,0:T(8,128)S(1)} %copy-done.1, f32[1,40,1024]{2,1,0:T(8,128)S(1)} %copy-done.2, f32[1,40,40]{2,1,0:T(8,128)S(1)} %copy-done.3, s32[1,1,16,128]{3,2,1,0:T(8,128)S(1)} %copy-done.4, ...), custom_call_target="tpu_custom_call" | custom-call | flops 1000000000 | bytes 11000000 | tf_op jit(solution)/shard_map/pallas_call | solution.py:292
  36.0 2.4 %copy.12 = f32[1,32,40,1024]{3,2,1,0:T(8,128)} copy(f32[1,32,40,1024]{3,2,1,0:T(8,128)S(1)} %get-tuple-element.4) | data formatting | bytes 10485760
  38.4 0.7 %copy.13 = f32[1,32,1024]{2,1,0:T(8,128)} copy(f32[1,32,1024]{2,1,0:T(8,128)S(1)} %get-tuple-element.5) | data formatting | bytes 262144
Async XLA Ops:
  0.6 2.5 %copy-start = (f32[1,32,40,1024]{3,2,1,0:T(8,128)S(1)}, f32[1,32,40,1024]{3,2,1,0:T(8,128)}, u32[]{:S(2)}) copy-start(f32[1,32,40,1024]{3,2,1,0:T(8,128)} %state.1) | copy-start | bytes 15728644
  3.1 0.9 %copy-start.1 = (f32[1,40,1024]{2,1,0:T(8,128)S(1)}, f32[1,40,1024]{2,1,0:T(8,128)}, u32[]{:S(2)}) copy-start(f32[1,40,1024]{2,1,0:T(8,128)} %diffusion.1) | copy-start | bytes 491524
  4.0 0.9 %copy-start.2 = (f32[1,40,1024]{2,1,0:T(8,128)S(1)}, f32[1,40,1024]{2,1,0:T(8,128)}, u32[]{:S(2)}) copy-start(f32[1,40,1024]{2,1,0:T(8,128)} %transport.1) | copy-start | bytes 491524
  5.0 0.7 %copy-start.3 = (f32[1,40,40]{2,1,0:T(8,128)S(1)}, f32[1,40,40]{2,1,0:T(8,128)}, u32[]{:S(2)}) copy-start(f32[1,40,40]{2,1,0:T(8,128)} %mixing.1) | copy-start | bytes 19204
  5.7 0.7 %copy-start.4 = (s32[1,1,16,128]{3,2,1,0:T(8,128)S(1)}, s32[1,1,16,128]{3,2,1,0:T(8,128)}, u32[]{:S(2)}) copy-start(s32[1,1,16,128]{3,2,1,0:T(8,128)} %src_col.1) | copy-start | bytes 24580
  6.4 0.7 %copy-start.5 = (f32[1,1,16,128]{3,2,1,0:T(8,128)S(1)}, f32[1,1,16,128]{3,2,1,0:T(8,128)}, u32[]{:S(2)}) copy-start(f32[1,1,16,128]{3,2,1,0:T(8,128)} %weights.1) | copy-start | bytes 24580
  7.1 0.7 %copy-start.6 = (s32[1,1,16,128]{3,2,1,0:T(8,128)S(1)}, s32[1,1,16,128]{3,2,1,0:T(8,128)}, u32[]{:S(2)}) copy-start(s32[1,1,16,128]{3,2,1,0:T(8,128)} %recv_rows.1) | copy-start | bytes 24580
  7.8 0.7 %copy-start.7 = (s32[1,1,16]{2,1,0:T(1,128)S(1)}, s32[1,1,16]{2,1,0:T(1,128)}, u32[]{:S(2)}) copy-start(s32[1,1,16]{2,1,0:T(1,128)} %counts.1) | copy-start | bytes 196

commit v2 on v1

--- a/solution.py
+++ b/solution.py
@@ -289,13 +289,17 @@
     edge = pltpu.VMEM((nlev, LANES), F32)
     rate = pltpu.VMEM((nlev, ncell), F32)
     dma = pltpu.SemaphoreType.DMA
+    inputs = [
+        pltpu.with_memory_space_constraint(x, pltpu.HBM)
+        for x in (state, diffusion, transport, mixing, src_col, weights, counts, recv_rows)
+    ]
     return pl.pallas_call(
         functools.partial(kernel, nblocks, prebuilt),
         out_shape=(
             jax.ShapeDtypeStruct(state.shape, F32),
             jax.ShapeDtypeStruct((1, nvar, ncell), F32),
         ),
-        in_specs=[pl.BlockSpec(memory_space=pl.ANY)] * 8,
+        in_specs=[pl.BlockSpec(memory_space=pltpu.HBM)] * 8,
         out_specs=[pl.BlockSpec(memory_space=pltpu.VMEM)] * 2,
         scratch_shapes=[
             pltpu.VMEM((nvar, nlev, ncell), F32),
@@ -322,7 +326,7 @@
         cost_estimate=pl.CostEstimate(
             flops=10**9, bytes_accessed=11 * 10**6, transcendentals=0
         ),
-    )(state, diffusion, transport, mixing, src_col, weights, counts, recv_rows)
+    )(*inputs)
 
 
 def solution(mesh):

time: 39.8 us -> 32.8 us (0.82); the launches traced: 39 us -> 32.6 us
  local copies, waits for them, and re-layouts: 10.8 us -> 3.02 us
  Pallas kernels: 27.6 us -> 28.9 us
    unnamed x18 -> x2, local copies, waits for them, and re-layouts: 10.8 us -> 3.02 us
    pallas_call x1, Pallas kernels: 27.6 us -> 28.9 us  [body(): pl.pallas_call(functools.partial(kernel, nblocks, prebuilt), out_shape=(j...]
where the time goes in v2:
time: 32.8 us; the launch traced here: 32.6 us
  Pallas kernels  28.9 us (88%)
  local copies, waits for them, and re-layouts  3.02 us (9%)
  between operations  0.64 us (2%)
    pallas_call x1, Pallas kernels, body(): pl.pallas_call(functools.partial(kernel, nblocks, prebuilt), out_shape=(j...  28.9 us
    unnamed x2, local copies, waits for them, and re-layouts  3.02 us

profile of v2, /device:TPU:1, one launch (start us, length us, event | category | flops | bytes accessed | tf_op | source)
XLA Modules:
  0.0 32.6 jit_solution(10157348962665556072)
XLA Ops:
  0.6 28.9 %shard_map.95 = (f32[1,32,40,1024]{3,2,1,0:T(8,128)S(1)}, f32[1,32,1024]{2,1,0:T(8,128)S(1)}) custom-call(f32[1,32,40,1024]{3,2,1,0:T(8,128)} %state.1, f32[1,40,1024]{2,1,0:T(8,128)} %diffusion.1, f32[1,40,1024]{2,1,0:T(8,128)} %transport.1, f32[1,40,40]{2,1,0:T(8,128)} %mixing.1, s32[1,1,16,128]{3,2,1,0:T(8,128)} %src_col.1, f32[1,1,16,128]{3,2,1,0:T(8,128)} %weights.1, ...), custom_call_target="tpu_custom_call" | custom-call | flops 1000000000 | bytes 11000000 | tf_op jit(solution)/shard_map/pallas_call | solution.py:296
  29.6 2.4 %copy.12 = f32[1,32,40,1024]{3,2,1,0:T(8,128)} copy(f32[1,32,40,1024]{3,2,1,0:T(8,128)S(1)} %get-tuple-element.4) | data formatting | bytes 10485760
  31.9 0.7 %copy.13 = f32[1,32,1024]{2,1,0:T(8,128)} copy(f32[1,32,1024]{2,1,0:T(8,128)S(1)} %get-tuple-element.5) | data formatting | bytes 262144

commit v3 on v2

--- a/solution.py
+++ b/solution.py
@@ -10,7 +10,8 @@
 MESH = pl.DeviceIdType.MESH
 F32 = jnp.float32
 BF16 = jnp.bfloat16
-GROUP = 2
+GROUP = 4
+UNROLL = 1
 CHUNKS = 4
 LANES = 128
 SELECTOR_BYTES = 8 << 20
@@ -41,7 +42,7 @@
     state, diffusion, transport, mixing, src_col, weights, counts, recv_rows,
     out, incoming,
     u, dif, tra, mix, src, wgt, cnt, rec,
-    rate_a, rate_b, rate_d, edge_l, edge_r, msg_l, msg_r, from_l, from_r,
+    coef, level_mix, edge_l, edge_r, msg_l, msg_r, from_l, from_r,
     surf, sendbuf, recvbuf, total, picker, placer,
     chunk_sem, small_sem, halo_send, halo_recv, send_sem, recv_sem,
 ):
@@ -103,9 +104,14 @@
     cell = lanes_of((nlev, ncell))
     d_all = dif[...]
     b_all = d_all + tra[...]
-    rate_a[...] = 1.0 - d_all - b_all
-    rate_b[...] = jnp.where(cell == 0, 0.0, b_all)
-    rate_d[...] = jnp.where(cell == ncell - 1, 0.0, d_all)
+    a_all = 1.0 - d_all - b_all
+    b_in = jnp.where(cell == 0, 0.0, b_all)
+    d_in = jnp.where(cell == ncell - 1, 0.0, d_all)
+    coef[0] = b_in * pltpu.roll(b_in, 1, 1)
+    coef[1] = b_in * (a_all + pltpu.roll(a_all, 1, 1))
+    coef[2] = a_all * a_all + b_in * pltpu.roll(d_in, 1, 1) + d_in * pltpu.roll(b_in, ncell - 1, 1)
+    coef[3] = d_in * (a_all + pltpu.roll(a_all, ncell - 1, 1))
+    coef[4] = d_in * pltpu.roll(d_in, ncell - 1, 1)
     d_first, d_last = dif[:, :LANES], dif[:, ncell - LANES :]
     b_first = d_first + tra[:, :LANES]
     b_last = d_last + tra[:, ncell - LANES :]
@@ -160,17 +166,21 @@
     top_mix = column_of(mix[0:1, :], nlev)
     top_mix = top_mix + jnp.where(rows_of((nlev, 1)) == 0, 1.0, 0.0)
 
-    @pl.loop(0, nvar)
+    level_mix[...] = jnp.broadcast_to(top_mix, level_mix.shape)
+
+    @pl.loop(0, nvar, unroll=UNROLL)
     def transport_substeps(v):
         acc = jnp.zeros((8, ncell), F32)
         for g in range(nlev // 8):
             span = slice(8 * g, 8 * g + 8)
-            a, b, d = rate_a[span, :], rate_b[span, :], rate_d[span, :]
-            x = u[v, span, :]
-            for step in range(2):
-                x = a * x + b * pltpu.roll(x, 1, 1) + d * pltpu.roll(x, ncell - 1, 1)
+            old = u[v, span, :]
+            x = coef[2, span, :] * old
+            for k, shift in enumerate((2, 1, 0, ncell - 1, ncell - 2)):
+                if shift:
+                    x = x + coef[k, span, :] * pltpu.roll(old, shift, 1)
             u[v, span, :] = x
-            acc = acc + top_mix[span, :] * x
+            scale = level_mix[span, :]
+            acc = acc + jnp.concatenate([scale] * (ncell // LANES), axis=1) * x
         surf[pl.ds(v, 1), :] = jnp.sum(acc, axis=0, keepdims=True)
 
     to_right.wait()
@@ -280,6 +290,21 @@
         contribution(d).wait_send()
 
 
+def write_out(column, arrived, new_state, incoming, sems):
+    per = column.shape[1] // CHUNKS
+    copies = [
+        pltpu.make_async_copy(
+            column.at[0, pl.ds(i * per, per)], new_state.at[0, pl.ds(i * per, per)], sems.at[i]
+        )
+        for i in range(CHUNKS)
+    ]
+    copies.append(pltpu.make_async_copy(arrived, incoming, sems.at[CHUNKS]))
+    for copy in copies:
+        copy.start()
+    for copy in copies:
+        copy.wait()
+
+
 def body(state, diffusion, transport, mixing, src_col, weights, counts, recv_rows):
     _, nvar, nlev, ncell = state.shape
     nblocks, nslot = src_col.shape[2:]
@@ -293,12 +318,13 @@
         pltpu.with_memory_space_constraint(x, pltpu.HBM)
         for x in (state, diffusion, transport, mixing, src_col, weights, counts, recv_rows)
     ]
-    return pl.pallas_call(
+    shapes = (
+        jax.ShapeDtypeStruct(state.shape, F32),
+        jax.ShapeDtypeStruct((1, nvar, ncell), F32),
+    )
+    column, arrived = pl.pallas_call(
         functools.partial(kernel, nblocks, prebuilt),
-        out_shape=(
-            jax.ShapeDtypeStruct(state.shape, F32),
-            jax.ShapeDtypeStruct((1, nvar, ncell), F32),
-        ),
+        out_shape=shapes,
         in_specs=[pl.BlockSpec(memory_space=pltpu.HBM)] * 8,
         out_specs=[pl.BlockSpec(memory_space=pltpu.VMEM)] * 2,
         scratch_shapes=[
@@ -309,8 +335,8 @@
             pltpu.VMEM((nblocks, nslot), F32),
             pltpu.VMEM((1, nblocks), jnp.int32),
             pltpu.VMEM((nblocks, nslot), jnp.int32),
-            rate, rate, rate,
-            edge, edge, edge, edge, edge, edge,
+            pltpu.VMEM((5, nlev, ncell), F32),
+            edge, edge, edge, edge, edge, edge, edge,
             pltpu.VMEM((nvar, ncell), F32),
             pltpu.VMEM((nblocks, nvar, nslot), F32),
             pltpu.VMEM((nblocks, nvar, nslot), F32),
@@ -327,6 +353,16 @@
             flops=10**9, bytes_accessed=11 * 10**6, transcendentals=0
         ),
     )(*inputs)
+    return tuple(
+        pl.pallas_call(
+            write_out,
+            out_shape=shapes,
+            in_specs=[pl.BlockSpec(memory_space=pl.ANY)] * 2,
+            out_specs=[pl.BlockSpec(memory_space=pl.ANY)] * 2,
+            scratch_shapes=[dma((CHUNKS + 1,))],
+            compiler_params=pltpu.CompilerParams(vmem_limit_bytes=40 << 20),
+        )(column, arrived)
+    )
 
 
 def solution(mesh):

time: 32.8 us -> 29.9 us (0.912)
  local copies, waits for them, and re-layouts: 3.02 us -> 0 us
    unnamed x2 -> x0, local copies, waits for them, and re-layouts: 3.02 us -> none
    pallas_call x1 -> x2, Pallas kernels: 28.9 us -> 29 us  [the longest x1 26.6 us: body(): pl.pallas_call(functools.partial(kernel, nblocks, prebuilt), out_shape=sh...]
where the time goes in v3:
time: 29.9 us; the launch traced here: 29.7 us
  Pallas kernels  29 us (97%)
  between operations  0.64 us (2%)
    pallas_call x1, Pallas kernels, body(): pl.pallas_call(functools.partial(kernel, nblocks, prebuilt), out_shape=sh...  26.6 us
    pallas_call x1, Pallas kernels, body(): pl.pallas_call(write_out, out_shape=shapes, in_specs=[pl.BlockSpec(memory...  2.43 us

profile of v3, /device:TPU:1, one launch (start us, length us, event | category | flops | bytes accessed | tf_op | source)
XLA Modules:
  0.0 29.7 jit_solution(5849615779570537092)
XLA Ops:
  0.6 26.6 %shard_map.95 = (f32[1,32,40,1024]{3,2,1,0:T(8,128)S(1)}, f32[1,32,1024]{2,1,0:T(8,128)S(1)}) custom-call(f32[1,32,40,1024]{3,2,1,0:T(8,128)} %state.1, f32[1,40,1024]{2,1,0:T(8,128)} %diffusion.1, f32[1,40,1024]{2,1,0:T(8,128)} %transport.1, f32[1,40,40]{2,1,0:T(8,128)} %mixing.1, s32[1,1,16,128]{3,2,1,0:T(8,128)} %src_col.1, f32[1,1,16,128]{3,2,1,0:T(8,128)} %weights.1, ...), custom_call_target="tpu_custom_call" | custom-call | flops 1000000000 | bytes 11000000 | tf_op jit(solution)/shard_map/pallas_call | solution.py:325
  27.2 2.4 %shard_map.96 = (f32[1,32,40,1024]{3,2,1,0:T(8,128)}, f32[1,32,1024]{2,1,0:T(8,128)}) custom-call(f32[1,32,40,1024]{3,2,1,0:T(8,128)S(1)} %get-tuple-element.4.column, f32[1,32,1024]{2,1,0:T(8,128)S(1)} %get-tuple-element.5.arrived), custom_call_target="tpu_custom_call" | custom-call | tf_op jit(solution)/shard_map/pallas_call | solution.py:357

commit v4 on v3

--- a/solution.py
+++ b/solution.py
@@ -11,7 +11,6 @@
 F32 = jnp.float32
 BF16 = jnp.bfloat16
 GROUP = 4
-UNROLL = 1
 CHUNKS = 4
 LANES = 128
 SELECTOR_BYTES = 8 << 20
@@ -168,20 +167,38 @@
 
     level_mix[...] = jnp.broadcast_to(top_mix, level_mix.shape)
 
-    @pl.loop(0, nvar, unroll=UNROLL)
-    def transport_substeps(v):
-        acc = jnp.zeros((8, ncell), F32)
+    count = ncell // LANES
+
+    @pl.loop(0, nvar // 2)
+    def transport_substeps(pair):
+        acc = [[jnp.zeros((8, LANES), F32)] * count for _ in range(2)]
         for g in range(nlev // 8):
             span = slice(8 * g, 8 * g + 8)
-            old = u[v, span, :]
-            x = coef[2, span, :] * old
-            for k, shift in enumerate((2, 1, 0, ncell - 1, ncell - 2)):
-                if shift:
-                    x = x + coef[k, span, :] * pltpu.roll(old, shift, 1)
-            u[v, span, :] = x
             scale = level_mix[span, :]
-            acc = acc + jnp.concatenate([scale] * (ncell // LANES), axis=1) * x
-        surf[pl.ds(v, 1), :] = jnp.sum(acc, axis=0, keepdims=True)
+            old = [u[2 * pair + w, span, :] for w in range(2)]
+            turned = [
+                {
+                    shift: pltpu.roll(x, shift % ncell, 1)
+                    for shift in (2, 1, -1, -2)
+                }
+                for x in old
+            ]
+            new = [[], []]
+            for i in range(count):
+                at = slice(i * LANES, (i + 1) * LANES)
+                rates = [coef[k, span, at] for k in range(5)]
+                for w in range(2):
+                    y = rates[2] * old[w][:, at]
+                    for k, shift in ((0, 2), (1, 1), (3, -1), (4, -2)):
+                        y = y + rates[k] * turned[w][shift][:, at]
+                    new[w].append(y)
+                    acc[w][i] = acc[w][i] + scale * y
+            for w in range(2):
+                u[2 * pair + w, span, :] = jnp.concatenate(new[w], axis=1)
+        for w in range(2):
+            surf[pl.ds(2 * pair + w, 1), :] = jnp.sum(
+                jnp.concatenate(acc[w], axis=1), axis=0, keepdims=True
+            )
 
     to_right.wait()
     to_left.wait()

time: 29.9 us -> 28.6 us (0.957)
  Pallas kernels: 29 us -> 27.8 us
    pallas_call x1, Pallas kernels: 26.6 us -> 25.4 us  [body(): pl.pallas_call(functools.partial(kernel, nblocks, prebuilt), out_shape=sh...]
where the time goes in v4:
time: 28.6 us; the launch traced here: 28.4 us
  Pallas kernels  27.8 us (97%)
  between operations  0.64 us (2%)
    pallas_call x1, Pallas kernels, body(): pl.pallas_call(functools.partial(kernel, nblocks, prebuilt), out_shape=sh...  25.4 us
    pallas_call x1, Pallas kernels, body(): pl.pallas_call(write_out, out_shape=shapes, in_specs=[pl.BlockSpec(memory...  2.43 us

profile of v4, /device:TPU:1, one launch (start us, length us, event | category | flops | bytes accessed | tf_op | source)
XLA Modules:
  0.0 28.4 jit_solution(697587369294638879)
XLA Ops:
  0.6 25.4 %shard_map.95 = (f32[1,32,40,1024]{3,2,1,0:T(8,128)S(1)}, f32[1,32,1024]{2,1,0:T(8,128)S(1)}) custom-call(f32[1,32,40,1024]{3,2,1,0:T(8,128)} %state.1, f32[1,40,1024]{2,1,0:T(8,128)} %diffusion.1, f32[1,40,1024]{2,1,0:T(8,128)} %transport.1, f32[1,40,40]{2,1,0:T(8,128)} %mixing.1, s32[1,1,16,128]{3,2,1,0:T(8,128)} %src_col.1, f32[1,1,16,128]{3,2,1,0:T(8,128)} %weights.1, ...), custom_call_target="tpu_custom_call" | custom-call | flops 1000000000 | bytes 11000000 | tf_op jit(solution)/shard_map/pallas_call | solution.py:342
  26.0 2.4 %shard_map.96 = (f32[1,32,40,1024]{3,2,1,0:T(8,128)}, f32[1,32,1024]{2,1,0:T(8,128)}) custom-call(f32[1,32,40,1024]{3,2,1,0:T(8,128)S(1)} %get-tuple-element.4.column, f32[1,32,1024]{2,1,0:T(8,128)S(1)} %get-tuple-element.5.arrived), custom_call_target="tpu_custom_call" | custom-call | tf_op jit(solution)/shard_map/pallas_call | solution.py:374
